TPU v7x, 128 devices: a whole 4x4x4 slice. The times are simulated.
128 devices in a mesh: tm: 64 (over z, y, x), seq: 2 (over core).
Axes of the slice: x: 4, y: 4, z: 4, core: 2. Of those that a mesh axis runs over, the one named last changes fastest.
Arguments:
- starts: float32 [64, 64, 1024], P('tm', None, 'seq'), may hold values from -6 to 6
- w_embed: bfloat16 [64, 2432], replicated, may hold values from -0.75 to 0.75
- pos_embed: bfloat16 [1024, 2432], replicated, may hold values from -5 to 5
- mod_table: float32 [64, 3, 2432], replicated, may hold values from -5 to 5
- mod_index: int32 [64, 2], P('tm'), may hold values from 0 to 63
- w_qkv: bfloat16 [2432, 3, 1536], P(None, None, 'seq'), may hold values from -0.15625 to 0.15625
- w_out: bfloat16 [1536, 2432], P('seq'), may hold values from -0.15625 to 0.15625
- text_kv: bfloat16 [2, 333, 1536], P(None, None, 'seq'), may hold values from -160 to 160
- w_final: bfloat16 [2432, 64], replicated, may hold values from -0.3125 to 0.3125
Outputs:
- corrected: float32 [64, 64, 1024], P('tm', None, 'seq')
- first_velocity: float32 [64, 64, 1024], P('tm', None, 'seq')
All inputs are finite; a program needn't handle non-finite values.
Results may differ from a plain program's by a relative error of at most 0.02.
The roundings to bfloat16 on the way count: a program that leaves them out, or rounds other values in their place, can miss the bound.
Values may be sent and summed in bfloat16 or wider, within the bound.
A program may use at most 192 MiB of HBM per device.

v0:
```python
import jax
import jax.numpy as jnp
from jax import lax
from jax.sharding import PartitionSpec as P

HD = 64


def layer_norm(values):
    row_mean = jnp.mean(values, -1, keepdims=True)
    centered = values - row_mean
    variance = jnp.mean(centered * centered, -1, keepdims=True)
    return centered * lax.rsqrt(variance + 1e-06)


def attention(projected, text_keys, text_values, head_cols):
    token_count = projected.shape[0]
    head_count = head_cols // HD
    queries = projected[:, :head_cols]
    key_rows = jnp.concatenate([projected[:, head_cols : 2 * head_cols], text_keys], 0).reshape(
        -1, head_count, HD
    )
    value_rows = jnp.concatenate([projected[:, 2 * head_cols :], text_values], 0).reshape(
        -1, head_count, HD
    )
    query_block = min(512, token_count)
    grouped = queries.reshape(token_count // query_block, query_block, head_count, HD)

    def attend(query_part):
        scores = jnp.einsum(
            "qhd,khd->hqk", query_part, key_rows, preferred_element_type=jnp.float32
        ) * HD ** (-0.5)
        row_max = jnp.max(scores, -1, keepdims=True)
        expanded = jnp.exp(scores - row_max)
        probs = (expanded / jnp.sum(expanded, -1, keepdims=True)).astype(jnp.bfloat16)
        result = jnp.einsum("hqk,khd->qhd", probs, value_rows, preferred_element_type=jnp.float32)
        return result.astype(jnp.bfloat16).reshape(query_block, head_cols)

    return lax.map(attend, grouped).reshape(token_count, head_cols)


def on_device(starts, w_embed, pos_embed, mod_table, mod_index, w_qkv, w_out, text_kv, w_final):
    blocks = lax.axis_size("tm")
    own_block = lax.axis_index("tm")
    token_share = starts.shape[2]
    head_cols = w_qkv.shape[2]
    model_width = w_embed.shape[1]
    levels = mod_table.shape[0]
    fine_steps = mod_index.shape[1]
    qkv_flat = w_qkv.reshape(model_width, 3 * head_cols)
    onehot = (mod_index[0][:, None] == jnp.arange(levels, dtype=jnp.int32)[None, :]).astype(
        jnp.float32
    )
    mod_rows = jnp.dot(
        onehot, mod_table.reshape(levels, 3 * model_width), precision=lax.Precision.HIGHEST
    )
    mod_rows = mod_rows.reshape(fine_steps, 3, model_width)
    offset = lax.axis_index("seq") * token_share
    pos_own = lax.dynamic_slice_in_dim(pos_embed, offset, token_share, 0).astype(jnp.float32)
    step_total = blocks * fine_steps

    def moment(step_index):
        grid_value = step_index.astype(jnp.float32)
        shifted = 1.0 - 0.95 * grid_value / step_total
        return 3.0 * shifted / (1.0 + 2.0 * shifted)

    block_start = starts[0]
    latent_state = block_start
    first_velocity = None
    for substep in range(fine_steps):
        conditioning = mod_rows[substep]
        shift_row = conditioning[0]
        scale_row = conditioning[1]
        gate_row = conditioning[2]
        latent = latent_state.astype(jnp.bfloat16)
        embedded = lax.dot_general(
            lax.all_gather(latent, "seq", axis=1, tiled=True),
            w_embed,
            (((0,), (0,)), ((), ())),
            preferred_element_type=jnp.float32,
        )
        embedded = embedded + pos_embed.astype(jnp.float32)
        modulated = (layer_norm(embedded) * (1.0 + scale_row) + shift_row).astype(jnp.bfloat16)
        projected = jnp.dot(modulated, qkv_flat, preferred_element_type=jnp.float32).astype(
            jnp.bfloat16
        )
        attended = attention(projected, text_kv[0], text_kv[1], head_cols)
        own_embedded = (
            lax.dot_general(
                latent, w_embed, (((0,), (0,)), ((), ())), preferred_element_type=jnp.float32
            )
            + pos_own
        )
        mixed_out = lax.psum_scatter(
            jnp.dot(attended, w_out, preferred_element_type=jnp.float32).astype(jnp.bfloat16),
            "seq",
            scatter_dimension=0,
            tiled=True,
        ).astype(jnp.float32)
        hidden = own_embedded + gate_row * mixed_out
        normed = layer_norm(hidden).astype(jnp.bfloat16)
        speed = lax.dot_general(
            w_final, normed, (((0,), (1,)), ((), ())), preferred_element_type=jnp.float32
        )
        if substep == 0:
            first_velocity = speed
        step_index = own_block * fine_steps + substep
        latent_state = latent_state + (moment(step_index + 1) - moment(step_index)) * speed
    decay_ratio = moment((own_block + 1) * fine_steps) / moment(own_block * fine_steps)
    correction = latent_state - decay_ratio * block_start
    decay_in = jnp.where(own_block == 0, 0.0, decay_ratio).reshape(1, 1)
    shift_in = jnp.where(own_block == 0, latent_state, correction)
    decay_all, shift_all = (
        lax.all_gather(decay_in[None], "tm", axis=0, tiled=True),
        lax.all_gather(shift_in[None], "tm", axis=0, tiled=True),
    )

    def advance(block_index, carried):
        moved = decay_all[block_index] * carried + shift_all[block_index]
        return jnp.where(block_index < own_block, moved, carried)

    new_start = lax.fori_loop(0, blocks, advance, block_start)
    corrected = decay_ratio * new_start + correction
    return (corrected[None], first_velocity[None])


def solution(mesh):
    placed = (
        P("tm", None, "seq"),
        P(),
        P(),
        P(),
        P("tm", None),
        P(None, None, "seq"),
        P("seq", None),
        P(None, None, "seq"),
        P(),
    )
    return jax.shard_map(
        on_device,
        mesh=mesh,
        in_specs=placed,
        out_specs=(P("tm", None, "seq"), P("tm", None, "seq")),
        check_vma=False,
    )
```

profile of v0, /device:TPU:0, one launch (start us, length us, event | category | flops | bytes accessed | tf_op | source)
XLA Modules:
  0.0 640.4 jit_solution(17259498010130303308)
XLA Ops:
  8.8 1.9 all_gather.13
  10.7 4.0 fusion.92
  15.9 2.9 copy-done.1
  20.3 14.8 %copy.20 = bf16[2432,3,768]{0,2,1:T(8,128)(2,1)} copy(bf16[2432,3,768]{2,0,1:T(8,128)(2,1)} %param.20) | data formatting | bytes 22413312 | tf_op args[5]
  35.1 18.7 %convolution_convert_fusion.3 = bf16[1024,2304]{1,0:T(8,128)(2,1)S(1)} fusion(bf16[2432,2304]{0,1:T(8,128)(2,1)} %bitcast.126, f32[1024,2432]{1,0:T(8,128)} %copy-done.1, f32[2432]{0:T(1024)S(1)} %get-tuple-element.176, f32[2432]{0:T(1024)S(1)} %get-tuple-element.177, f32[1024]{0:T(1024)S(1)} %add_rsqrt_fusion.1, f32[1024]{0:T(1024)S(1)} %broadcast_multiply_fusion.1), kind=kOutput, calls=%fused_computation.50 | convolution fusion | flops 11490426880 | bytes 25914368 | tf_op jit(solution)/shard_map/dot_general | solution.py:84
  55.3 2.6 copy.22
  57.9 1.6 copy.24
  59.5 3.9 fusion.91
  63.4 3.1 copy.23
  66.4 2.0 copy.25
  70.6 3.9 pad_maximum_fusion.1
  75.8 65.2 %while.33 = (s32[]{:T(128)}, bf16[2,512,768]{2,1,0:T(8,128)(2,1)}, bf16[2,512,12,64]{1,3,2,0:T(8,128)(2,1)S(1)}, bf16[1357,12,64]{0,2,1:T(8,128)(2,1)}, bf16[1357,12,64]{0,2,1:T(8,128)(2,1)}, /*index=5*/s32[]{:T(128)}) while((s32[]{:T(128)}, bf16[2,512,768]{2,1,0:T(8,128)(2,1)}, bf16[2,512,12,64]{1,3,2,0:T(8,128)(2,1)S(1)}, ...), condition=%wide.region_5.6_spmd, body=%wide.region_2.5_spmd.sunk | while | flops 2176458240 | bytes 75636296 | solution.py:39
  76.0 18.5 %fusion.133 = (f32[12,512]{1,0:T(8,128)S(1)}, f32[12,512,1357]{1,2,0:T(8,128)}) fusion(bf16[1357,12,64]{0,2,1:T(8,128)(2,1)} %get-tuple-element.351, bf16[2,512,12,64]{1,3,2,0:T(8,128)(2,1)S(1)} %get-tuple-element.350, s32[]{:T(128)} %get-tuple-element.342), kind=kOutput, calls=%fused_computation.105.clone.1 | convolution fusion | flops 1092201856 | bytes 36244996 | tf_op jit(solution)/shard_map/while/body/eval_jaxpr/sub | solution.py:34
  94.5 12.8 %fusion.134 = bf16[12,512,64]{1,2,0:T(8,128)(2,1)S(1)} fusion(bf16[1357,12,64]{0,2,1:T(8,128)(2,1)} %get-tuple-element.352, f32[12,512,1357]{1,2,0:T(8,128)} %get-tuple-element.322, f32[12,512]{1,0:T(8,128)S(1)} %get-tuple-element.323), kind=kOutput, calls=%fused_computation.8.clone.1 | convolution fusion | flops 1084256256 | bytes 36244992 | tf_op jit(solution)/shard_map/while/body/eval_jaxpr/hqk,khd->qhd/dot_general | solution.py:36
  108.5 18.5 %fusion.133 = (f32[12,512]{1,0:T(8,128)S(1)}, f32[12,512,1357]{1,2,0:T(8,128)}) fusion(bf16[1357,12,64]{0,2,1:T(8,128)(2,1)} %get-tuple-element.351, bf16[2,512,12,64]{1,3,2,0:T(8,128)(2,1)S(1)} %get-tuple-element.350, s32[]{:T(128)} %get-tuple-element.342), kind=kOutput, calls=%fused_computation.105.clone.1 | convolution fusion | flops 1092201856 | bytes 36244996 | tf_op jit(solution)/shard_map/while/body/eval_jaxpr/sub | solution.py:34
  127.0 12.8 %fusion.134 = bf16[12,512,64]{1,2,0:T(8,128)(2,1)S(1)} fusion(bf16[1357,12,64]{0,2,1:T(8,128)(2,1)} %get-tuple-element.352, f32[12,512,1357]{1,2,0:T(8,128)} %get-tuple-element.322, f32[12,512]{1,0:T(8,128)S(1)} %get-tuple-element.323), kind=kOutput, calls=%fused_computation.8.clone.1 | convolution fusion | flops 1084256256 | bytes 36244992 | tf_op jit(solution)/shard_map/while/body/eval_jaxpr/hqk,khd->qhd/dot_general | solution.py:36
  141.0 9.0 %convolution_convert_fusion.1 = bf16[1024,2432]{1,0:T(8,128)(2,1)} fusion(bf16[1024,768]{1,0:T(8,128)(2,1)} %bitcast.140, bf16[768,2432]{1,0:T(8,128)(2,1)} %param.21), kind=kOutput, calls=%fused_computation.48 | convolution fusion | flops 3827695616 | bytes 10289152 | tf_op jit(solution)/shard_map/dot_general | solution.py:95
  150.4 17.7 %reduce-scatter.3.cloned.1.call-done = bf16[512,2432]{1,0:T(8,128)(2,1)} async-done(((bf16[1024,2432]{1,0:T(8,128)(2,1)}), bf16[512,2432]{1,0:T(8,128)(2,1)}) %reduce-scatter.3.cloned.1.call-update) | async-done | bytes 2490384 | tf_op jit(solution)/shard_map/reduce_scatter | solution.py:94
  168.1 3.8 fusion.93
  173.0 1.7 fusion.72
  175.3 1.9 all_gather.14
  180.0 16.2 %convolution_convert_fusion.2 = bf16[1024,2304]{1,0:T(8,128)(2,1)S(1)} fusion(bf16[2432,2304]{0,1:T(8,128)(2,1)} %bitcast.127, f32[1024,2432]{1,0:T(8,128)S(1)} %get-tuple-element.228, f32[2432]{0:T(1024)S(1)} %copy-done.14, f32[2432]{0:T(1024)S(1)} %copy-done.15, f32[1024]{0:T(1024)S(1)} %add_rsqrt_fusion, f32[1024]{0:T(1024)S(1)} %broadcast_multiply_fusion), kind=kOutput, calls=%fused_computation.49 | convolution fusion | flops 11490426880 | bytes 25914368 | tf_op jit(solution)/shard_map/dot_general | solution.py:84
  197.6 2.6 copy.29
  200.2 3.2 pad_maximum_fusion
  203.4 1.6 copy.30
  205.0 3.2 pad_maximum_fusion.2
  211.8 65.3 %while.34 = (s32[]{:T(128)}, bf16[2,512,768]{2,1,0:T(8,128)(2,1)}, bf16[2,512,12,64]{1,3,2,0:T(8,128)(2,1)S(1)}, bf16[1357,12,64]{0,2,1:T(8,128)(2,1)}, bf16[1357,12,64]{0,2,1:T(8,128)(2,1)}, /*index=5*/s32[]{:T(128)}) while((s32[]{:T(128)}, bf16[2,512,768]{2,1,0:T(8,128)(2,1)}, bf16[2,512,12,64]{1,3,2,0:T(8,128)(2,1)S(1)}, ...), condition=%wide.region_14.15_spmd, body=%wide.region_11.14_spmd.sunk | while | flops 2176458240 | bytes 75636296 | solution.py:39
  212.0 18.5 %fusion.138 = (f32[12,512]{1,0:T(8,128)S(1)}, f32[12,512,1357]{1,2,0:T(8,128)}) fusion(bf16[1357,12,64]{0,2,1:T(8,128)(2,1)} %get-tuple-element.369, bf16[2,512,12,64]{1,3,2,0:T(8,128)(2,1)S(1)} %get-tuple-element.368, s32[]{:T(128)} %get-tuple-element.360), kind=kOutput, calls=%fused_computation.106.clone.1 | convolution fusion | flops 1092201856 | bytes 36244996 | tf_op jit(solution)/shard_map/while/body/eval_jaxpr/sub | solution.py:34
  230.5 12.8 %fusion.139 = bf16[12,512,64]{1,2,0:T(8,128)(2,1)S(1)} fusion(bf16[1357,12,64]{0,2,1:T(8,128)(2,1)} %get-tuple-element.370, f32[12,512,1357]{1,2,0:T(8,128)} %get-tuple-element.329, f32[12,512]{1,0:T(8,128)S(1)} %get-tuple-element.330), kind=kOutput, calls=%fused_computation.26.clone.1 | convolution fusion | flops 1084256256 | bytes 36244992 | tf_op jit(solution)/shard_map/while/body/eval_jaxpr/hqk,khd->qhd/dot_general | solution.py:36
  244.5 18.5 %fusion.138 = (f32[12,512]{1,0:T(8,128)S(1)}, f32[12,512,1357]{1,2,0:T(8,128)}) fusion(bf16[1357,12,64]{0,2,1:T(8,128)(2,1)} %get-tuple-element.369, bf16[2,512,12,64]{1,3,2,0:T(8,128)(2,1)S(1)} %get-tuple-element.368, s32[]{:T(128)} %get-tuple-element.360), kind=kOutput, calls=%fused_computation.106.clone.1 | convolution fusion | flops 1092201856 | bytes 36244996 | tf_op jit(solution)/shard_map/while/body/eval_jaxpr/sub | solution.py:34
  263.0 12.8 %fusion.139 = bf16[12,512,64]{1,2,0:T(8,128)(2,1)S(1)} fusion(bf16[1357,12,64]{0,2,1:T(8,128)(2,1)} %get-tuple-element.370, f32[12,512,1357]{1,2,0:T(8,128)} %get-tuple-element.329, f32[12,512]{1,0:T(8,128)S(1)} %get-tuple-element.330), kind=kOutput, calls=%fused_computation.26.clone.1 | convolution fusion | flops 1084256256 | bytes 36244992 | tf_op jit(solution)/shard_map/while/body/eval_jaxpr/hqk,khd->qhd/dot_general | solution.py:36
  277.1 9.0 %convolution_convert_fusion = bf16[1024,2432]{1,0:T(8,128)(2,1)} fusion(bf16[1024,768]{1,0:T(8,128)(2,1)} %bitcast.139, bf16[768,2432]{1,0:T(8,128)(2,1)} %param.21), kind=kOutput, calls=%fused_computation.47 | convolution fusion | flops 3827695616 | bytes 10289152 | tf_op jit(solution)/shard_map/dot_general | solution.py:95
  286.5 16.7 %reduce-scatter.5.cloned.1.call-done = bf16[512,2432]{1,0:T(8,128)(2,1)} async-done(((bf16[1024,2432]{1,0:T(8,128)(2,1)}), bf16[512,2432]{1,0:T(8,128)(2,1)}) %reduce-scatter.5.cloned.1.call-update) | async-done | bytes 2490384 | tf_op jit(solution)/shard_map/reduce_scatter | solution.py:94
  303.3 3.7 fusion.95
  308.1 1.8 fusion.71
  311.3 180.1 %all-reduce = f32[64]{0:T(128)S(1)} all-reduce(f32[64]{0:T(128)S(1)} %dynamic-update-slice), channel_id=1, replica_groups=mesh['tm'=64,'seq'=2] {'tm'}, use_global_device_ids=true, to_apply=%add | all-reduce | flops 64 | bytes 512
  491.4 141.3 %while.35 = (s32[]{:T(128)}, f32[64,512]{1,0:T(8,128)S(1)}, s32[]{:T(128)}, f32[64,1,1]{0,2,1:T(1,128)S(1)}, f32[64,64,512]{2,1,0:T(8,128)}, /*index=5*/s32[]{:T(128)}) while((s32[]{:T(128)}, f32[64,512]{1,0:T(8,128)S(1)}, s32[]{:T(128)}, f32[64,1,1]{0,2,1:T(1,128)S(1)}, f32[64,64,512]{2,1,0:T(8,128)}, /*index=5*/s32[]{:T(128)}) %tuple.101), condition=%wide.region_19.20_spmd, body=%wide.region_18.19_spmd.sunk | while | flops 98307 | bytes 393315 | solution.py:122
  492.0 1.6 fusion.140
  494.2 1.6 fusion.140
  496.4 1.6 fusion.140
  498.6 1.6 fusion.140
  503.1 1.6 fusion.140
  505.3 1.6 fusion.140
  507.5 1.6 fusion.140
  509.7 1.6 fusion.140
  511.9 1.6 fusion.140
  514.1 1.6 fusion.140
  518.5 1.6 fusion.140
  520.7 1.6 fusion.140
  522.9 1.6 fusion.140
  525.1 1.6 fusion.140
  527.3 1.6 fusion.140
  529.5 1.6 fusion.140
  534.0 1.6 fusion.140
  536.2 1.6 fusion.140
  538.4 1.6 fusion.140
  540.6 1.6 fusion.140
  545.0 1.6 fusion.140
  547.2 1.6 fusion.140
  549.4 1.6 fusion.140
  551.6 1.6 fusion.140
  553.8 1.6 fusion.140
  556.0 1.6 fusion.140
  560.4 1.6 fusion.140
  (188 shorter events, 124.1 us)
Async XLA Ops:
  7.2 3.5 copy-start
  7.2 160.9 %reduce-scatter.3.cloned.1.call-start = ((), (), s32[]{:S(2)}) async-start(), calls=%async_computation.2 | async-start | bytes 7471104 | tf_op jit(solution)/shard_map/reduce_scatter | solution.py:94
  8.2 0.6 copy-start.9
  14.7 4.0 copy-start.1
  14.7 4.0 copy-start.4
  14.7 4.1 copy-start.16
  150.0 18.1 %copy-start.10 = (bf16[64,512]{1,0:T(8,128)(2,1)S(1)}, bf16[64,512]{1,0:T(8,128)(2,1)}, u32[]{:S(2)}) copy-start(bf16[64,512]{1,0:T(8,128)(2,1)} %copy-done.9) | copy-start | bytes 196612
  150.0 18.1 %copy-start.13 = (f32[2432]{0:T(1024)S(1)}, f32[2432]{0:T(1024)}, u32[]{:S(2)}) copy-start(f32[2432]{0:T(1024)} %get-tuple-element.178) | copy-start | bytes 29188
  150.0 153.3 %reduce-scatter.5.cloned.1.call-start = ((), (), s32[]{:S(2)}) async-start(), calls=%async_computation.3 | async-start | bytes 7471104 | tf_op jit(solution)/shard_map/reduce_scatter | solution.py:94
  168.1 9.1 %slice-start = ((s8[4980736]{0:T(1024)(128)(4,1)}), s8[4194304]{0:T(1024)(128)(4,1)S(1)}, s32[]{:S(2)}) async-start(s8[4980736]{0:T(1024)(128)(4,1)} %bitcast.122), calls=%async_computation.5 | async-start | bytes 8388608
  171.9 0.9 copy-start.2
  171.9 1.0 copy-start.5
  172.0 5.2 slice-start.1
  174.7 0.6 copy-start.7
  178.8 1.2 copy-start.14
  178.8 1.2 copy-start.15
  286.0 17.2 %copy-start.8 = (bf16[64,512]{1,0:T(8,128)(2,1)S(1)}, bf16[64,512]{1,0:T(8,128)(2,1)}, u32[]{:S(2)}) copy-start(bf16[64,512]{1,0:T(8,128)(2,1)} %copy-done.7) | copy-start | bytes 196612
  286.0 17.2 %copy-start.12 = (f32[2432]{0:T(1024)S(1)}, f32[2432]{0:T(1024)}, u32[]{:S(2)}) copy-start(f32[2432]{0:T(1024)} %get-tuple-element.173) | copy-start | bytes 29188
  286.1 205.3 %all-gather.3.cloned.1.call-start = ((), (), s32[]{:S(2)}) async-start(), calls=%async_computation.4 | async-start | bytes 8519680 | tf_op jit(solution)/shard_map/all_gather | solution.py:115
  307.0 0.9 copy-start.3
  307.0 1.0 copy-start.6
  307.0 1.0 copy-start.11
  307.0 2.9 copy-start.17
Sparse Core Ops, SparseCore 0:
  150.1 17.9 reduce-scatter.2
  286.2 17.0 reduce-scatter.4
  310.0 80.6 all-gather.2
where the time goes:
time: 651 us; the launch traced here: 640 us
  matrix products  195 us (30%)
  blocking collectives  184 us (28%)
  other arithmetic  119 us (18%)
  local copies, waits for them, and re-layouts  90.9 us (14%)
  waiting for transfers between devices  34.5 us (5%)
  between operations  14.8 us (2%)
    unnamed x1, blocking collectives  180 us
    select_n x64, other arithmetic, advance(): return jnp.where(block_index < own_block, moved, carried)  103 us
    sub x4, matrix products, attend(): expanded = jnp.exp(scores - row_max)  74 us
    dot_general x4, matrix products, attend(): jnp.einsum('hqk,khd->qhd', probs, value_rows, preferred_element_type=jnp....  51.1 us
    dynamic_slice x64, local copies, waits for them, and re-layouts, advance(): moved = decay_all[block_index] * carried + shift_all[block_index]  37.4 us
    dot_general x2, matrix products, on_device(): jnp.dot(modulated, qkv_flat, preferred_element_type=jnp.float32)  34.8 us
    reduce_scatter x2, waiting for transfers between devices, on_device(): lax.psum_scatter(jnp.dot(attended, w_out, preferred_element_type=jnp.floa...  34.5 us
    unnamed x45, local copies, waits for them, and re-layouts  21.1 us
  transfers between devices with their start and end apart: 3, of which 2 were waited for; matrix products, arithmetic and copies ran while one was open for 0% of the time, Pallas kernels for 0%

commit v1 on v0

v1 whole, which is shorter than its diff:
```python
import functools
import math

import jax
import jax.numpy as jnp
from jax import lax
from jax.experimental import pallas as pl
from jax.experimental.pallas import tpu as pltpu
from jax.sharding import PartitionSpec as P

HD = 64
MESH = pl.DeviceIdType.MESH
F32 = jnp.float32
BF16 = jnp.bfloat16
TN = (((0,), (0,)), ((), ()))
NT = (((1,), (1,)), ((), ()))
RING = 4


def moment(step_index, step_total):
    shifted = 1.0 - 0.95 * step_index.astype(F32) / step_total
    return 3.0 * shifted / (1.0 + 2.0 * shifted)


def normalized(values):
    centered = values - jnp.mean(values, -1, keepdims=True)
    variance = jnp.mean(centered * centered, -1, keepdims=True)
    return centered * lax.rsqrt(variance + 1e-06)


def span(index, size, align):
    return pl.ds(pl.multiple_of(index * size, align), size)


def kernel(
    key_total,
    starts,
    w_embed,
    pos_hbm,
    mod_table,
    mod_index,
    w_qkv_hbm,
    w_out_hbm,
    text,
    w_final,
    corrected,
    first_velocity,
    pos,
    w_qkv,
    w_out,
    latents,
    state,
    modulated,
    queries,
    keys,
    values,
    scores_a,
    scores_b,
    attended,
    sums_out,
    sums_in,
    load_sem,
    latent_send,
    latent_recv,
    att_send,
    att_recv,
    wide_send,
    wide_recv,
    scan_send,
    scan_recv,
):
    own_block = lax.axis_index("tm")
    own = lax.axis_index("seq")
    blocks = lax.axis_size("tm")
    peer = {"tm": own_block, "seq": 1 - own}
    share = starts.shape[1]
    image = 2 * share
    head_cols = w_out_hbm.shape[0]
    heads = head_cols // HD
    fine_steps = mod_index.shape[1]
    step_total = blocks * fine_steps
    own_tokens = span(own, share, share)

    ring_axes = []
    for stride in (1, RING, RING * RING):
        place = (own_block // stride) % RING
        peers = []
        for distance in range(1, RING):
            target = own_block + ((place + distance) % RING - place) * stride
            peers.append({"tm": target, "seq": own})
        ring_axes.append((place, peers))

    barrier = pltpu.get_barrier_semaphore()
    greeted = [peer] + [device for _, peers in ring_axes for device in peers]
    for device in greeted:
        pl.semaphore_signal(barrier, inc=1, device_id=device, device_id_type=MESH)

    loads = [pltpu.make_async_copy(pos_hbm, pos, load_sem.at[0])]
    for part in range(3):
        loads.append(
            pltpu.make_async_copy(
                w_qkv_hbm.at[part], w_qkv.at[part], load_sem.at[1 + part]
            )
        )
    loads.append(pltpu.make_async_copy(w_out_hbm, w_out.at[0], load_sem.at[4]))
    for load in loads:
        load.start()

    state[...] = starts[...]
    latents[0, :, own_tokens] = starts[...].astype(BF16)
    pl.semaphore_wait(barrier, len(greeted))

    def latent_copy(step):
        return pltpu.make_async_remote_copy(
            src_ref=latents.at[step, :, own_tokens],
            dst_ref=latents.at[step, :, own_tokens],
            send_sem=latent_send.at[step],
            recv_sem=latent_recv.at[step],
            device_id=peer,
            device_id_type=MESH,
        )

    def attended_copy(step):
        return pltpu.make_async_remote_copy(
            src_ref=attended.at[0],
            dst_ref=attended.at[2],
            send_sem=att_send.at[step],
            recv_sem=att_recv.at[step],
            device_id=peer,
            device_id_type=MESH,
        )

    latent_copy(0).start()
    wide_copy = pltpu.make_async_remote_copy(
        src_ref=w_out_hbm,
        dst_ref=w_out.at[1],
        send_sem=wide_send,
        recv_sem=wide_recv,
        device_id=peer,
        device_id_type=MESH,
    )
    wide_copy.start()

    text_rows = text.shape[0]
    keys[image : image + text_rows, :] = text[:, :head_cols]
    values[:, image : image + text_rows] = text[:, head_cols:].T

    lane = lax.broadcasted_iota(jnp.int32, (1, 2 * HD), 1)
    key_row = lax.broadcasted_iota(jnp.int32, (8, 1), 0)
    key_rows = keys.shape[0]

    def score(index, buffer):
        index = jnp.minimum(index, 2 * heads - 1)
        tile = jnp.where(index < heads, 1 - own, own)
        head = index % heads
        pair = span(head // 2, 2 * HD, 2 * HD)
        query = queries[span(tile, share, share), pair]
        query = jnp.where(lane // HD == head % 2, query, jnp.zeros_like(query))
        buffer[...] = lax.dot_general(keys[:, pair], query, NT, preferred_element_type=F32)
        buffer[key_rows - 8 :, :] = jnp.where(
            key_row < key_total - (key_rows - 8), buffer[key_rows - 8 :, :], -1e30
        )

    def attend(index, buffer):
        head = index % heads
        rows = span(head, HD, HD)
        value = buffer[...]
        expanded = jnp.exp2(value - jnp.max(value, axis=0, keepdims=True))
        total = jnp.sum(expanded, axis=0, keepdims=True)
        result = jnp.dot(values[rows, :], expanded.astype(BF16), preferred_element_type=F32)
        attended[index // heads, rows, :] = (result / total).astype(BF16)

    def fine_step(step, carry):
        level = mod_index[0, step]
        shift = mod_table[0, pl.ds(level, 1), :]
        scale = 1.0 + mod_table[1, pl.ds(level, 1), :]
        gate = mod_table[2, pl.ds(level, 1), :]

        @pl.when(step == 0)
        def _():
            loads[0].wait()

        chunk = 256
        chunks = image // chunk

        def embed(tokens):
            embedded = lax.dot_general(
                latents[step, :, tokens], w_embed[...], TN, preferred_element_type=F32
            )
            return embedded + pos[tokens, :].astype(F32)

        def modulate(index, carry):
            @pl.when(index == chunks // 2)
            def _():
                latent_copy(step).wait_recv()

            tokens = span((own * (chunks // 2) + index) % chunks, chunk, chunk)
            modulated[tokens, :] = (normalized(embed(tokens)) * scale + shift).astype(BF16)
            return carry

        lax.fori_loop(0, chunks, modulate, 0)
        latent_copy(step).wait_send()

        @pl.when(step == 0)
        def _():
            for load in loads[1:4]:
                load.wait()

        def project(part):
            return jnp.dot(modulated[...], w_qkv[part], preferred_element_type=F32)

        queries[...] = (project(0) * (HD**-0.5 / math.log(2))).astype(BF16)
        keys[:image, :] = project(1).astype(BF16)
        values[:, :image] = project(2).astype(BF16).T

        score(0, scores_a)

        def pair_of_heads(index, carry):
            score(2 * index + 1, scores_b)
            attend(2 * index, scores_a)
            score(2 * index + 2, scores_a)
            attend(2 * index + 1, scores_b)
            return carry

        lax.fori_loop(0, heads // 2, pair_of_heads, 0)
        attended_copy(step).start()
        lax.fori_loop(heads // 2, heads, pair_of_heads, 0)
        attended_copy(step).wait()

        @pl.when(step == 0)
        def _():
            loads[4].wait()
            wide_copy.wait()

        fine_index = own_block * fine_steps + step
        pace = moment(fine_index + 1, step_total) - moment(fine_index, step_total)

        def finish(index, carry):
            within = span(index, chunk, chunk)
            tokens = span(own * (share // chunk) + index, chunk, chunk)
            mixed = lax.dot_general(
                attended[1, :, within], w_out[0], TN, preferred_element_type=F32
            ) + lax.dot_general(attended[2, :, within], w_out[1], TN, preferred_element_type=F32)
            hidden = embed(tokens) + gate * mixed
            normed = normalized(hidden).astype(BF16)
            speed = lax.dot_general(w_final[...], normed, NT, preferred_element_type=F32)
            state[:, within] = state[:, within] + pace * speed

            @pl.when(step == 0)
            def _():
                first_velocity[:, within] = speed

            return carry

        lax.fori_loop(0, share // chunk, finish, 0)

        @pl.when(step < fine_steps - 1)
        def _():
            latents[step + 1, :, own_tokens] = state[...].astype(BF16)
            latent_copy(step + 1).start()

        return carry

    lax.fori_loop(0, fine_steps, fine_step, 0)

    time_before = moment(own_block * fine_steps, step_total)
    time_after = moment((own_block + 1) * fine_steps, step_total)
    keep_start = jnp.where(own_block == 0, 0.0, 1.0)
    share_sum = state[...] / time_after - (keep_start / time_before) * starts[...]
    result = share_sum
    for axis, (place, peers) in enumerate(ring_axes):
        sums_out[axis] = share_sum.astype(BF16)
        copies = []
        for slot, device in enumerate(peers):
            copy = pltpu.make_async_remote_copy(
                src_ref=sums_out.at[axis],
                dst_ref=sums_in.at[axis, slot],
                send_sem=scan_send.at[axis, slot],
                recv_sem=scan_recv.at[axis, slot],
                device_id=device,
                device_id_type=MESH,
            )
            copy.start()
            copies.append(copy)
        for slot, copy in enumerate(copies):
            copy.wait()
            arrived = sums_in[axis, slot].astype(F32)
            earlier = jnp.where(place >= slot + 1, 1.0, 0.0)
            result = result + earlier * arrived
            share_sum = share_sum + arrived
    corrected[...] = time_after * result


def on_device(starts, w_embed, pos_embed, mod_table, mod_index, w_qkv, w_out, text_kv, w_final):
    channels, share = starts.shape[1:]
    image, width = pos_embed.shape
    head_cols = w_out.shape[0]
    text_total = text_kv.shape[1]
    text_rows = -(-text_total // 16) * 16
    key_rows = image + text_rows
    text = text_kv.transpose(1, 0, 2).reshape(text_total, 2 * head_cols)
    text = jnp.pad(text, ((0, text_rows - text_total), (0, 0)))
    vmem = pl.BlockSpec(memory_space=pltpu.VMEM)
    anywhere = pl.BlockSpec(memory_space=pl.ANY)
    corrected, first_velocity = pl.pallas_call(
        functools.partial(kernel, image + text_total),
        out_shape=[jax.ShapeDtypeStruct((channels, share), F32)] * 2,
        in_specs=[
            vmem,
            vmem,
            anywhere,
            vmem,
            pl.BlockSpec(memory_space=pltpu.SMEM),
            anywhere,
            anywhere,
            vmem,
            vmem,
        ],
        out_specs=[vmem, vmem],
        scratch_shapes=[
            pltpu.VMEM((image, width), BF16),
            pltpu.VMEM((3, width, head_cols), BF16),
            pltpu.VMEM((2, head_cols, width), BF16),
            pltpu.VMEM((2, channels, image), BF16),
            pltpu.VMEM((channels, share), F32),
            pltpu.VMEM((image, width), BF16),
            pltpu.VMEM((image, head_cols), BF16),
            pltpu.VMEM((key_rows, head_cols), BF16),
            pltpu.VMEM((head_cols, key_rows), BF16),
            pltpu.VMEM((key_rows, share), F32),
            pltpu.VMEM((key_rows, share), F32),
            pltpu.VMEM((3, head_cols, share), BF16),
            pltpu.VMEM((3, channels, share), BF16),
            pltpu.VMEM((3, RING - 1, channels, share), BF16),
            pltpu.SemaphoreType.DMA((5,)),
            pltpu.SemaphoreType.DMA((2,)),
            pltpu.SemaphoreType.DMA((2,)),
            pltpu.SemaphoreType.DMA((2,)),
            pltpu.SemaphoreType.DMA((2,)),
            pltpu.SemaphoreType.DMA,
            pltpu.SemaphoreType.DMA,
            pltpu.SemaphoreType.DMA((3, RING - 1)),
            pltpu.SemaphoreType.DMA((3, RING - 1)),
        ],
        compiler_params=pltpu.CompilerParams(
            collective_id=0, has_side_effects=True, vmem_limit_bytes=60 << 20
        ),
    )(
        starts[0],
        w_embed,
        pos_embed,
        mod_table.transpose(1, 0, 2),
        mod_index,
        w_qkv.transpose(1, 0, 2),
        w_out,
        text,
        w_final.T,
    )
    return corrected[None], first_velocity[None]


def solution(mesh):
    placed = (
        P("tm", None, "seq"),
        P(),
        P(),
        P(),
        P("tm", None),
        P(None, None, "seq"),
        P("seq", None),
        P(None, None, "seq"),
        P(),
    )
    return jax.shard_map(
        on_device,
        mesh=mesh,
        in_specs=placed,
        out_specs=(P("tm", None, "seq"), P("tm", None, "seq")),
        check_vma=False,
    )
```

time: 651 us -> 125 us (0.19); the launches traced: 640 us -> 125 us
  matrix products: 195 us -> 0 us
  blocking collectives: 184 us -> 0 us
  other arithmetic: 119 us -> 0 us
  Pallas kernels: 0 us -> 118 us
  local copies, waits for them, and re-layouts: 90.9 us -> 6.34 us
  waiting for transfers between devices: 34.5 us -> 0 us
  between operations: 14.8 us -> 0.65 us
    unnamed x1 -> x0, blocking collectives: 180 us -> none
    dot_general x15 -> x0, matrix products: 121 us -> none  [the longest x4 51.1 us: attend(): jnp.einsum('hqk,khd->qhd', probs, value_rows, preferred_element_type=jnp....]
    pallas_call x0 -> x1, Pallas kernels: none -> 118 us  [on_device(): pl.pallas_call(functools.partial(kernel, image + text_total), out_shape=[...]
    select_n x64 -> x0, other arithmetic: 103 us -> none  [advance(): return jnp.where(block_index < own_block, moved, carried)]
    sub x4 -> x0, matrix products: 74 us -> none  [attend(): expanded = jnp.exp(scores - row_max)]
    dynamic_slice x64 -> x0, local copies, waits for them, and re-layouts: 37.4 us -> none  [advance(): moved = decay_all[block_index] * carried + shift_all[block_index]]
    reduce_scatter x2 -> x0, waiting for transfers between devices: 34.5 us -> none  [on_device(): lax.psum_scatter(jnp.dot(attended, w_out, preferred_element_type=jnp.floa...]
    slice x11 -> x0, local copies, waits for them, and re-layouts: 21.8 us -> none  [the longest x3 8.88 us: on_device(): attended = attention(projected, text_kv[0], text_kv[1], head_cols)]
  transfers between devices with their start and end apart: 3 -> 0, of which waited for: 2 -> 0; matrix products, arithmetic and copies ran while one was open for 0% -> 0% of each run, Pallas kernels for 0% -> 0%
where the time goes in v1:
time: 125 us
  Pallas kernels  118 us (94%)
  local copies, waits for them, and re-layouts  6.34 us (5%)
    pallas_call x1, Pallas kernels, on_device(): pl.pallas_call(functools.partial(kernel, image + text_total), out_shape=[...  118 us
    unnamed x4, local copies, waits for them, and re-layouts  5.28 us

profile of v1, /device:TPU:0, one launch (start us, length us, event | category | flops | bytes accessed | tf_op | source)
XLA Modules:
  0.0 124.8 jit_solution(7851441632849246507)
XLA Ops:
  0.6 2.0 %pad.5 = bf16[336,2,768]{2,1,0:T(2,128)(2,1)S(1)} pad(bf16[333,2,768]{2,1,0:T(2,128)(2,1)} %bitcast.14, bf16[]{:T(256)} %constant.2.clone.1), padding=0_3x0_0x0_0 | pad | bytes 2055170
  2.6 0.1 copy.11
  2.8 1.1 pad.4.text
  3.8 117.8 %shard_map.104 = (f32[64,512]{1,0:T(8,128)}, f32[64,512]{1,0:T(8,128)}) custom-call(f32[64,512]{1,0:T(8,128)} %bitcast.16, bf16[64,2432]{1,0:T(8,128)(2,1)} %w_embed.1, bf16[1024,2432]{1,0:T(8,128)(2,1)} %pos_hbm.1, f32[3,64,2432]{2,1,0:T(8,128)} %bitcast.13, s32[1,2]{1,0:T(1,128)} %mod_index.1, bf16[3,2432,768]{2,1,0:T(8,128)(2,1)} %bitcast.10, ...), custom_call_target="tpu_custom_call" | custom-call | tf_op jit(solution)/shard_map/pallas_call | solution.py:305
  121.7 1.6 %copy.14 = f32[1,64,512]{2,1,0:T(8,128)} copy(f32[1,64,512]{2,1,0:T(8,128)} %bitcast.18) | data formatting | bytes 262144
  123.3 1.6 %copy.15 = f32[1,64,512]{2,1,0:T(8,128)} copy(f32[1,64,512]{2,1,0:T(8,128)} %bitcast.17) | data formatting | bytes 262144

commit v2 on v1

v2 whole, which is shorter than its diff:
```python
import functools
import math

import jax
import jax.numpy as jnp
from jax import lax
from jax.experimental import pallas as pl
from jax.experimental.pallas import tpu as pltpu
from jax.sharding import PartitionSpec as P

HD = 64
MESH = pl.DeviceIdType.MESH
F32 = jnp.float32
BF16 = jnp.bfloat16
TN = (((0,), (0,)), ((), ()))
NT = (((1,), (1,)), ((), ()))
RING = 4
EXTRA = 16


def moment(step_index, step_total):
    shifted = 1.0 - 0.95 * step_index.astype(F32) / step_total
    return 3.0 * shifted / (1.0 + 2.0 * shifted)


def split_rows(row):
    parts = []
    for _ in range(3):
        part = row.astype(BF16).astype(F32)
        parts.append(part)
        row = row - part
    parts.append(jnp.zeros((EXTRA - 3, row.shape[1]), F32))
    return jnp.concatenate(parts, axis=0).astype(BF16)


def span(index, size, align):
    return pl.ds(pl.multiple_of(index * size, align), size)


def kernel(
    key_total,
    starts,
    w_embed_hbm,
    pos_hbm,
    mod_table_hbm,
    mod_index,
    w_qkv_hbm,
    w_out_hbm,
    text_hbm,
    w_final_hbm,
    corrected,
    first_velocity,
    w_embed,
    w_embed_t,
    w_sums,
    pos,
    pos_t,
    pos_sums,
    hidden,
    work,
    mod_table,
    gate_t,
    w_qkv,
    w_out,
    w_out_t,
    text,
    w_final,
    latents,
    state,
    modulated,
    queries,
    keys,
    values,
    scores_a,
    scores_b,
    attended,
    sums_out,
    sums_in,
    load_sem,
    ready_sem,
    latent_send,
    latent_recv,
    att_send,
    att_recv,
    wide_send,
    wide_recv,
    scan_send,
    scan_recv,
):
    own_block = lax.axis_index("tm")
    own = lax.axis_index("seq")
    blocks = lax.axis_size("tm")
    peer = {"tm": own_block, "seq": 1 - own}
    channels, share = starts.shape
    image = 2 * share
    head_cols = w_out_hbm.shape[0]
    heads = head_cols // HD
    fine_steps = mod_index.shape[1]
    step_total = blocks * fine_steps
    own_tokens = span(own, share, share)

    ring_axes = []
    for stride in (1, RING, RING * RING):
        place = (own_block // stride) % RING
        peers = []
        for distance in range(1, RING):
            target = own_block + ((place + distance) % RING - place) * stride
            peers.append({"tm": target, "seq": own})
        ring_axes.append((place, peers))

    barrier = pltpu.get_barrier_semaphore()
    pl.semaphore_signal(barrier, inc=1, device_id=peer, device_id_type=MESH)

    def for_peers(higher, action):
        for place, peers in ring_axes:
            for distance, device in enumerate(peers, 1):
                above = place + distance < RING

                @pl.when(above if higher else jnp.logical_not(above))
                def _():
                    action(device)

    def greet(device):
        pl.semaphore_signal(barrier, inc=1, device_id=device, device_id_type=MESH)

    def answer(device):
        pl.semaphore_signal(ready_sem, inc=1, device_id=device, device_id_type=MESH)

    for_peers(True, greet)
    below = sum([place for place, _ in ring_axes], jnp.int32(0))
    above_total = (RING - 1) * len(ring_axes) - below

    chunk = 256
    chunks = image // chunk
    half = chunks // 2
    width = pos.shape[1]
    third = -(-width // 48) * 16
    out_cuts = [0, third, 2 * third, width]

    def ordered(index):
        return span((own * half + index) % chunks, chunk, chunk)

    def load(source, target, index):
        copy = pltpu.make_async_copy(source, target, load_sem.at[index])
        return copy

    embed_loads = [load(w_embed_hbm, w_embed.at[:channels, :], 0), load(mod_table_hbm, mod_table, 1)]
    pos_loads = [
        load(pos_hbm.at[ordered(index), :], pos.at[ordered(index), :], 2 + index)
        for index in range(chunks)
    ]
    out_loads = [load(w_out_hbm, w_out, 6), load(text_hbm, text, 7), load(w_final_hbm, w_final, 8)]
    qkv_loads = [load(w_qkv_hbm.at[part], w_qkv.at[part], 9 + part) for part in range(3)]
    for copy in embed_loads + pos_loads + out_loads + qkv_loads:
        copy.start()

    state[...] = starts[...]
    latents[0, :, own_tokens] = starts[...].astype(BF16)
    pl.semaphore_wait(barrier, 1 + below)
    for_peers(False, answer)

    def latent_copy(step):
        return pltpu.make_async_remote_copy(
            src_ref=latents.at[step, :, own_tokens],
            dst_ref=latents.at[step, :, own_tokens],
            send_sem=latent_send.at[step],
            recv_sem=latent_recv.at[step],
            device_id=peer,
            device_id_type=MESH,
        )

    def attended_copy(step):
        return pltpu.make_async_remote_copy(
            src_ref=attended.at[:head_cols],
            dst_ref=attended.at[2 * head_cols :],
            send_sem=att_send.at[step],
            recv_sem=att_recv.at[step],
            device_id=peer,
            device_id_type=MESH,
        )

    latent_copy(0).start()
    wide_copy = pltpu.make_async_remote_copy(
        src_ref=w_out_t.at[:, :head_cols],
        dst_ref=w_out_t.at[:, head_cols:],
        send_sem=wide_send,
        recv_sem=wide_recv,
        device_id=peer,
        device_id_type=MESH,
    )
    for copy in embed_loads:
        copy.wait()
    w_embed_t[...] = w_embed[:channels, :].T
    w_embed[channels:, :] = jnp.ones((EXTRA, width), BF16)
    w_sums[...] = jnp.broadcast_to(
        jnp.sum(w_embed[:channels, :].astype(F32), axis=1, keepdims=True), (channels, 128)
    )

    lane = lax.broadcasted_iota(jnp.int32, (1, 2 * HD), 1)
    key_row = lax.broadcasted_iota(jnp.int32, (8, 1), 0)
    key_rows = keys.shape[0]

    def score(index, buffer):
        index = jnp.minimum(index, 2 * heads - 1)
        tile = jnp.where(index < heads, 1 - own, own)
        head = index % heads
        pair = span(head // 2, 2 * HD, 2 * HD)
        query = queries[span(tile, share, share), pair]
        query = jnp.where(lane // HD == head % 2, query, jnp.zeros_like(query))
        buffer[...] = lax.dot_general(keys[:, pair], query, NT, preferred_element_type=F32)
        buffer[key_rows - 8 :, :] = jnp.where(
            key_row < key_total - (key_rows - 8), buffer[key_rows - 8 :, :], -1e30
        )

    def attend(index, buffer):
        head = index % heads
        rows = span(head, HD, HD)
        value = buffer[...]
        expanded = jnp.exp2(value - jnp.max(value, axis=0, keepdims=True))
        total = jnp.sum(expanded, axis=0, keepdims=True)
        result = jnp.dot(values[rows, :], expanded.astype(BF16), preferred_element_type=F32)
        attended[span(index, HD, HD), :] = (result / total).astype(BF16)

    def fine_step(step, carry):
        level = mod_index[0, step]
        shift = mod_table[0, pl.ds(level, 1), :]
        scale = 1.0 + mod_table[1, pl.ds(level, 1), :]
        gate = mod_table[2, pl.ds(level, 1), :]

        def modulate(index, carry):
            @pl.when(step == 0)
            def _():
                for place in range(chunks):

                    @pl.when(index == place)
                    def _():
                        pos_loads[place].wait()

            @pl.when(index == half)
            def _():
                latent_copy(step).wait_recv()

            tokens = ordered(index)
            @pl.when(step == 0)
            def _():
                ones = jnp.ones((EXTRA, width), BF16)
                pos_sums[:, tokens] = lax.dot_general(
                    ones, pos[tokens, :], NT, preferred_element_type=F32
                )[:8]

            latent = latents[step, :, tokens]
            weight = jnp.concatenate([w_sums[...]] * (chunk // 128), axis=1)
            total = jnp.sum(latent.astype(F32) * weight, axis=0, keepdims=True)
            row_mean = (total + pos_sums[:1, tokens]) * (1.0 / width)
            work[...] = lax.dot_general(
                jnp.concatenate([latent, split_rows(-row_mean)], axis=0),
                w_embed[...],
                TN,
                preferred_element_type=F32,
            ) + pos[tokens, :].astype(F32)
            variance = jnp.mean(work[...] * work[...], axis=-1, keepdims=True)
            modulated[tokens, :] = (
                work[...] * lax.rsqrt(variance + 1e-06) * scale + shift
            ).astype(BF16)
            return carry

        lax.fori_loop(0, chunks, modulate, 0)
        latent_copy(step).wait_send()
        gate_t[...] = jnp.broadcast_to(gate, (128, width)).T

        @pl.when(step == 0)
        def _():
            for copy in out_loads:
                copy.wait()
            w_out_t[:, :head_cols] = w_out[...].T
            wide_copy.start()
            pos_t[...] = pos[own_tokens, :].T
            spare = key_rows - key_total
            both = text[...].astype(F32)
            blank = jnp.zeros((spare, head_cols), F32)
            keys[image:, :] = jnp.concatenate([both[:, 0, :], blank], axis=0).astype(BF16)
            value_rows = jnp.concatenate([both[:, 1, :], blank], axis=0).astype(BF16)
            values[:, image:] = value_rows.T
            for copy in qkv_loads:
                copy.wait()

        def project(part):
            return jnp.dot(modulated[...], w_qkv[part], preferred_element_type=F32)

        queries[...] = (project(0) * (HD**-0.5 / math.log(2))).astype(BF16)
        keys[:image, :] = project(1).astype(BF16)
        values[:, :image] = project(2).astype(BF16).T

        score(0, scores_a)

        def pair_of_heads(index, carry):
            score(2 * index + 1, scores_b)
            attend(2 * index, scores_a)
            score(2 * index + 2, scores_a)
            attend(2 * index + 1, scores_b)
            return carry

        lax.fori_loop(0, heads // 2, pair_of_heads, 0)
        attended_copy(step).start()
        lax.fori_loop(heads // 2, heads, pair_of_heads, 0)
        attended_copy(step).wait()

        @pl.when(step == 0)
        def _():
            wide_copy.wait()

        fine_index = own_block * fine_steps + step
        pace = moment(fine_index + 1, step_total) - moment(fine_index, step_total)

        gates = jnp.concatenate([gate_t[...]] * (share // 128), axis=1)
        middle = None
        first = jnp.zeros((1, share), F32)
        second = jnp.zeros((1, share), F32)
        for low, high in zip(out_cuts[:-1], out_cuts[1:]):
            rows = slice(low, high)
            mixed = jnp.dot(
                w_out_t[rows, :], attended[head_cols:, :], preferred_element_type=F32
            )
            embedded = jnp.dot(
                w_embed_t[rows, :], latents[step, :, own_tokens], preferred_element_type=F32
            )
            part = embedded + pos_t[rows, :].astype(F32) + gates[rows, :] * mixed
            hidden[rows, :] = part
            if middle is None:
                middle = jnp.mean(part, axis=0, keepdims=True)
            moved = hidden[rows, :] - middle
            first = first + jnp.sum(moved, axis=0, keepdims=True)
            second = second + jnp.sum(moved * moved, axis=0, keepdims=True)
        first = first * (1.0 / width)
        spread = lax.rsqrt(second * (1.0 / width) - first * first + 1e-06)
        normed = ((hidden[...] - (middle + first)) * spread).astype(BF16)
        speed = jnp.dot(w_final[...], normed, preferred_element_type=F32)
        state[...] = state[...] + pace * speed

        @pl.when(step == 0)
        def _():
            first_velocity[...] = speed

        @pl.when(step < fine_steps - 1)
        def _():
            latents[step + 1, :, own_tokens] = state[...].astype(BF16)
            latent_copy(step + 1).start()

        return carry

    lax.fori_loop(0, fine_steps, fine_step, 0)

    time_before = moment(own_block * fine_steps, step_total)
    time_after = moment((own_block + 1) * fine_steps, step_total)
    keep_start = jnp.where(own_block == 0, 0.0, 1.0)
    share_sum = state[...] / time_after - (keep_start / time_before) * starts[...]
    result = share_sum

    @pl.when(above_total > 0)
    def _():
        pl.semaphore_wait(ready_sem, above_total)

    for axis, (place, peers) in enumerate(ring_axes):
        upward = axis == len(ring_axes) - 1
        sums_out[axis] = share_sum.astype(BF16)
        copies = []
        for slot, device in enumerate(peers):
            copy = pltpu.make_async_remote_copy(
                src_ref=sums_out.at[axis],
                dst_ref=sums_in.at[axis, slot],
                send_sem=scan_send.at[axis, slot],
                recv_sem=scan_recv.at[axis, slot],
                device_id=device,
                device_id_type=MESH,
            )
            copies.append(copy)
            if upward:
                pl.when(place + slot + 1 < RING)(copy.start)
            else:
                copy.start()
        if upward:
            corrected[...] = result
        for slot, copy in enumerate(copies):
            if upward:

                @pl.when(place >= slot + 1)
                def _():
                    copy.wait_recv()
                    corrected[...] += sums_in[axis, slot].astype(F32)

            else:
                copy.wait()
                arrived = sums_in[axis, slot].astype(F32)
                earlier = jnp.where(place >= slot + 1, 1.0, 0.0)
                result = result + earlier * arrived
                share_sum = share_sum + arrived
        if upward:
            for slot, copy in enumerate(copies):
                pl.when(place + slot + 1 < RING)(copy.wait_send)
    corrected[...] = time_after * corrected[...]


def hand_over(corrected, first_velocity, corrected_out, first_velocity_out):
    corrected_out[0] = corrected[...]
    first_velocity_out[0] = first_velocity[...]


def on_device(starts, w_embed, pos_embed, mod_table, mod_index, w_qkv, w_out, text_kv, w_final):
    channels, share = starts.shape[1:]
    image, width = pos_embed.shape
    head_cols = w_out.shape[0]
    text_total = text_kv.shape[1]
    text_rows = -(-text_total // 16) * 16
    key_rows = image + text_rows
    text = text_kv.transpose(1, 0, 2)
    vmem = pl.BlockSpec(memory_space=pltpu.VMEM)
    anywhere = pl.BlockSpec(memory_space=pl.ANY)
    corrected, first_velocity = pl.pallas_call(
        functools.partial(kernel, image + text_total),
        out_shape=[jax.ShapeDtypeStruct((channels, share), F32)] * 2,
        in_specs=[
            vmem,
            anywhere,
            anywhere,
            anywhere,
            pl.BlockSpec(memory_space=pltpu.SMEM),
            anywhere,
            anywhere,
            anywhere,
            anywhere,
        ],
        out_specs=[vmem, vmem],
        scratch_shapes=[
            pltpu.VMEM((channels + EXTRA, width), BF16),
            pltpu.VMEM((width, channels), BF16),
            pltpu.VMEM((channels, 128), F32),
            pltpu.VMEM((image, width), BF16),
            pltpu.VMEM((width, share), BF16),
            pltpu.VMEM((8, image), F32),
            pltpu.VMEM((width, share), F32),
            pltpu.VMEM((256, width), F32),
            pltpu.VMEM((3, mod_table.shape[0], width), F32),
            pltpu.VMEM((width, 128), F32),
            pltpu.VMEM((3, width, head_cols), BF16),
            pltpu.VMEM((head_cols, width), BF16),
            pltpu.VMEM((width, 2 * head_cols), BF16),
            pltpu.VMEM((text_total, 2, head_cols), BF16),
            pltpu.VMEM((channels, width), BF16),
            pltpu.VMEM((2, channels, image), BF16),
            pltpu.VMEM((channels, share), F32),
            pltpu.VMEM((image, width), BF16),
            pltpu.VMEM((image, head_cols), BF16),
            pltpu.VMEM((key_rows, head_cols), BF16),
            pltpu.VMEM((head_cols, key_rows), BF16),
            pltpu.VMEM((key_rows, share), F32),
            pltpu.VMEM((key_rows, share), F32),
            pltpu.VMEM((3 * head_cols, share), BF16),
            pltpu.VMEM((3, channels, share), BF16),
            pltpu.VMEM((3, RING - 1, channels, share), BF16),
            pltpu.SemaphoreType.DMA((12,)),
            pltpu.SemaphoreType.REGULAR,
            pltpu.SemaphoreType.DMA((2,)),
            pltpu.SemaphoreType.DMA((2,)),
            pltpu.SemaphoreType.DMA((2,)),
            pltpu.SemaphoreType.DMA((2,)),
            pltpu.SemaphoreType.DMA,
            pltpu.SemaphoreType.DMA,
            pltpu.SemaphoreType.DMA((3, RING - 1)),
            pltpu.SemaphoreType.DMA((3, RING - 1)),
        ],
        compiler_params=pltpu.CompilerParams(
            collective_id=0, has_side_effects=True, vmem_limit_bytes=62 << 20
        ),
    )(
        starts[0],
        w_embed,
        pos_embed,
        mod_table.transpose(1, 0, 2),
        mod_index,
        w_qkv.transpose(1, 0, 2),
        w_out,
        text,
        w_final.T,
    )
    shape = jax.ShapeDtypeStruct((1, channels, share), F32)
    return pl.pallas_call(
        hand_over,
        out_shape=[shape] * 2,
        in_specs=[vmem, vmem],
        out_specs=[vmem, vmem],
    )(corrected, first_velocity)


def solution(mesh):
    placed = (
        P("tm", None, "seq"),
        P(),
        P(),
        P(),
        P("tm", None),
        P(None, None, "seq"),
        P("seq", None),
        P(None, None, "seq"),
        P(),
    )
    return jax.shard_map(
        on_device,
        mesh=mesh,
        in_specs=placed,
        out_specs=(P("tm", None, "seq"), P("tm", None, "seq")),
        check_vma=False,
    )
```

time: 125 us -> 112 us (0.90)
  Pallas kernels: 118 us -> 111 us
  local copies, waits for them, and re-layouts: 6.34 us -> 0 us
    pallas_call x1, Pallas kernels: 118 us -> 109 us  [on_device(): pl.pallas_call(functools.partial(kernel, image + text_total), out_shape=[...]
    unnamed x4 -> x0, local copies, waits for them, and re-layouts: 5.28 us -> none
    pallas_call x0 -> x1, Pallas kernels: none -> 1.68 us  [on_device(): pl.pallas_call(hand_over, out_shape=[shape] * 2, in_specs=[vmem, vmem], o...]
where the time goes in v2:
time: 112 us
  Pallas kernels  111 us (99%)
    pallas_call x1, Pallas kernels, on_device(): pl.pallas_call(functools.partial(kernel, image + text_total), out_shape=[...  109 us

profile of v2, /device:TPU:0, one launch (start us, length us, event | category | flops | bytes accessed | tf_op | source)
XLA Modules:
  0.0 111.8 jit_solution(848805235119736892)
XLA Ops:
  0.6 109.5 %shard_map.104 = (f32[64,512]{1,0:T(8,128)}, f32[64,512]{1,0:T(8,128)}) custom-call(f32[64,512]{1,0:T(8,128)} %bitcast.9, bf16[64,2432]{1,0:T(8,128)(2,1)} %w_embed_hbm.1, bf16[1024,2432]{1,0:T(8,128)(2,1)} %pos_hbm.1, f32[3,64,2432]{2,1,0:T(8,128)} %bitcast.6, s32[1,2]{1,0:T(1,128)} %mod_index.1, bf16[3,2432,768]{2,1,0:T(8,128)(2,1)} %bitcast.5, ...), custom_call_target="tpu_custom_call" | custom-call | tf_op jit(solution)/shard_map/pallas_call | solution.py:418
  110.1 1.7 %shard_map.105 = (f32[1,64,512]{2,1,0:T(8,128)}, f32[1,64,512]{2,1,0:T(8,128)}) custom-call(f32[64,512]{1,0:T(8,128)} %get-tuple-element.4.corrected, f32[64,512]{1,0:T(8,128)} %get-tuple-element.5.first_velocity), custom_call_target="tpu_custom_call" | custom-call | tf_op jit(solution)/shard_map/pallas_call | solution.py:486

commit v3 on v2

--- a/solution.py
+++ b/solution.py
@@ -57,7 +57,6 @@
     pos_t,
     pos_sums,
     hidden,
-    work,
     mod_table,
     gate_t,
     w_qkv,
@@ -196,18 +195,17 @@
         jnp.sum(w_embed[:channels, :].astype(F32), axis=1, keepdims=True), (channels, 128)
     )
 
-    lane = lax.broadcasted_iota(jnp.int32, (1, 2 * HD), 1)
+    feature = lax.broadcasted_iota(jnp.int32, (2 * HD, 1), 0)
     key_row = lax.broadcasted_iota(jnp.int32, (8, 1), 0)
     key_rows = keys.shape[0]
 
     def score(index, buffer):
-        index = jnp.minimum(index, 2 * heads - 1)
         tile = jnp.where(index < heads, 1 - own, own)
         head = index % heads
         pair = span(head // 2, 2 * HD, 2 * HD)
-        query = queries[span(tile, share, share), pair]
-        query = jnp.where(lane // HD == head % 2, query, jnp.zeros_like(query))
-        buffer[...] = lax.dot_general(keys[:, pair], query, NT, preferred_element_type=F32)
+        query = queries[pair, span(tile, share, share)]
+        query = jnp.where(feature // HD == head % 2, query, jnp.zeros_like(query))
+        buffer[...] = jnp.dot(keys[:, pair], query, preferred_element_type=F32)
         buffer[key_rows - 8 :, :] = jnp.where(
             key_row < key_total - (key_rows - 8), buffer[key_rows - 8 :, :], -1e30
         )
@@ -217,8 +215,10 @@
         rows = span(head, HD, HD)
         value = buffer[...]
         expanded = jnp.exp2(value - jnp.max(value, axis=0, keepdims=True))
-        total = jnp.sum(expanded, axis=0, keepdims=True)
-        result = jnp.dot(values[rows, :], expanded.astype(BF16), preferred_element_type=F32)
+        weights = jnp.concatenate([values[rows, :], jnp.ones((EXTRA, key_rows), BF16)], axis=0)
+        result = jnp.dot(weights, expanded.astype(BF16), preferred_element_type=F32)
+        total = result[HD : HD + 1]
+        result = result[:HD]
         attended[span(index, HD, HD), :] = (result / total).astype(BF16)
 
     def fine_step(step, carry):
@@ -252,15 +252,15 @@
             weight = jnp.concatenate([w_sums[...]] * (chunk // 128), axis=1)
             total = jnp.sum(latent.astype(F32) * weight, axis=0, keepdims=True)
             row_mean = (total + pos_sums[:1, tokens]) * (1.0 / width)
-            work[...] = lax.dot_general(
+            centered = lax.dot_general(
                 jnp.concatenate([latent, split_rows(-row_mean)], axis=0),
                 w_embed[...],
                 TN,
                 preferred_element_type=F32,
             ) + pos[tokens, :].astype(F32)
-            variance = jnp.mean(work[...] * work[...], axis=-1, keepdims=True)
+            variance = jnp.mean(centered * centered, axis=-1, keepdims=True)
             modulated[tokens, :] = (
-                work[...] * lax.rsqrt(variance + 1e-06) * scale + shift
+                centered * lax.rsqrt(variance + 1e-06) * scale + shift
             ).astype(BF16)
             return carry
 
@@ -287,7 +287,7 @@
         def project(part):
             return jnp.dot(modulated[...], w_qkv[part], preferred_element_type=F32)
 
-        queries[...] = (project(0) * (HD**-0.5 / math.log(2))).astype(BF16)
+        queries[...] = (project(0) * (HD**-0.5 / math.log(2))).astype(BF16).T
         keys[:image, :] = project(1).astype(BF16)
         values[:, :image] = project(2).astype(BF16).T
 
@@ -300,9 +300,14 @@
             attend(2 * index + 1, scores_b)
             return carry
 
-        lax.fori_loop(0, heads // 2, pair_of_heads, 0)
+        lax.fori_loop(0, heads // 2, pair_of_heads, 0, unroll=3)
         attended_copy(step).start()
-        lax.fori_loop(heads // 2, heads, pair_of_heads, 0)
+        lax.fori_loop(heads // 2, heads - 3, pair_of_heads, 0, unroll=3)
+        for index in range(heads - 3, heads - 1):
+            pair_of_heads(index, 0)
+        score(2 * heads - 1, scores_b)
+        attend(2 * heads - 2, scores_a)
+        attend(2 * heads - 1, scores_b)
         attended_copy(step).wait()
 
         @pl.when(step == 0)
@@ -362,11 +367,11 @@
 
     for axis, (place, peers) in enumerate(ring_axes):
         upward = axis == len(ring_axes) - 1
-        sums_out[axis] = share_sum.astype(BF16)
+        sums_out[...] = share_sum.astype(BF16)
         copies = []
         for slot, device in enumerate(peers):
             copy = pltpu.make_async_remote_copy(
-                src_ref=sums_out.at[axis],
+                src_ref=sums_out,
                 dst_ref=sums_in.at[axis, slot],
                 send_sem=scan_send.at[axis, slot],
                 recv_sem=scan_recv.at[axis, slot],
@@ -438,7 +443,6 @@
             pltpu.VMEM((width, share), BF16),
             pltpu.VMEM((8, image), F32),
             pltpu.VMEM((width, share), F32),
-            pltpu.VMEM((256, width), F32),
             pltpu.VMEM((3, mod_table.shape[0], width), F32),
             pltpu.VMEM((width, 128), F32),
             pltpu.VMEM((3, width, head_cols), BF16),
@@ -449,13 +453,13 @@
             pltpu.VMEM((2, channels, image), BF16),
             pltpu.VMEM((channels, share), F32),
             pltpu.VMEM((image, width), BF16),
-            pltpu.VMEM((image, head_cols), BF16),
+            pltpu.VMEM((head_cols, image), BF16),
             pltpu.VMEM((key_rows, head_cols), BF16),
             pltpu.VMEM((head_cols, key_rows), BF16),
             pltpu.VMEM((key_rows, share), F32),
             pltpu.VMEM((key_rows, share), F32),
             pltpu.VMEM((3 * head_cols, share), BF16),
-            pltpu.VMEM((3, channels, share), BF16),
+            pltpu.VMEM((channels, share), BF16),
             pltpu.VMEM((3, RING - 1, channels, share), BF16),
             pltpu.SemaphoreType.DMA((12,)),
             pltpu.SemaphoreType.REGULAR,
@@ -469,7 +473,7 @@
             pltpu.SemaphoreType.DMA((3, RING - 1)),
         ],
         compiler_params=pltpu.CompilerParams(
-            collective_id=0, has_side_effects=True, vmem_limit_bytes=62 << 20
+            collective_id=0, has_side_effects=True, vmem_limit_bytes=63 << 20
         ),
     )(
         starts[0],

time: 112 us -> 106 us (0.946)
  Pallas kernels: 111 us -> 105 us
    pallas_call x1, Pallas kernels: 109 us -> 103 us  [on_device(): pl.pallas_call(functools.partial(kernel, image + text_total), out_shape=[...]
where the time goes in v3:
time: 106 us
  Pallas kernels  105 us (99%)
    pallas_call x1, Pallas kernels, on_device(): pl.pallas_call(functools.partial(kernel, image + text_total), out_shape=[...  103 us

profile of v3, /device:TPU:0, one launch (start us, length us, event | category | flops | bytes accessed | tf_op | source)
XLA Modules:
  0.0 105.7 jit_solution(4598771215124553722)
XLA Ops:
  0.6 103.4 %shard_map.104 = (f32[64,512]{1,0:T(8,128)}, f32[64,512]{1,0:T(8,128)}) custom-call(f32[64,512]{1,0:T(8,128)} %bitcast.9, bf16[64,2432]{1,0:T(8,128)(2,1)} %w_embed_hbm.1, bf16[1024,2432]{1,0:T(8,128)(2,1)} %pos_hbm.1, f32[3,64,2432]{2,1,0:T(8,128)} %bitcast.6, s32[1,2]{1,0:T(1,128)} %mod_index.1, bf16[3,2432,768]{2,1,0:T(8,128)(2,1)} %bitcast.5, ...), custom_call_target="tpu_custom_call" | custom-call | tf_op jit(solution)/shard_map/pallas_call | solution.py:423
  104.1 1.7 %shard_map.105 = (f32[1,64,512]{2,1,0:T(8,128)}, f32[1,64,512]{2,1,0:T(8,128)}) custom-call(f32[64,512]{1,0:T(8,128)} %get-tuple-element.4.corrected, f32[64,512]{1,0:T(8,128)} %get-tuple-element.5.first_velocity), custom_call_target="tpu_custom_call" | custom-call | tf_op jit(solution)/shard_map/pallas_call | solution.py:490

commit v4 on v3

--- a/solution.py
+++ b/solution.py
@@ -149,7 +149,16 @@
         for index in range(chunks)
     ]
     out_loads = [load(w_out_hbm, w_out, 6), load(text_hbm, text, 7), load(w_final_hbm, w_final, 8)]
-    qkv_loads = [load(w_qkv_hbm.at[part], w_qkv.at[part], 9 + part) for part in range(3)]
+    quarter = width // 4
+    qkv_loads = [
+        load(
+            w_qkv_hbm.at[part, pl.ds(piece * quarter, quarter), :],
+            w_qkv.at[part, pl.ds(piece * quarter, quarter), :],
+            9 + 4 * part + piece,
+        )
+        for part in range(3)
+        for piece in range(4)
+    ]
     for copy in embed_loads + pos_loads + out_loads + qkv_loads:
         copy.start()
 
@@ -461,7 +470,7 @@
             pltpu.VMEM((3 * head_cols, share), BF16),
             pltpu.VMEM((channels, share), BF16),
             pltpu.VMEM((3, RING - 1, channels, share), BF16),
-            pltpu.SemaphoreType.DMA((12,)),
+            pltpu.SemaphoreType.DMA((21,)),
             pltpu.SemaphoreType.REGULAR,
             pltpu.SemaphoreType.DMA((2,)),
             pltpu.SemaphoreType.DMA((2,)),

time: 106 us -> 106 us (level)
  no operation moved by 1% of the time
where the time goes in v4:
time: 106 us
  Pallas kernels  105 us (99%)
    pallas_call x1, Pallas kernels, on_device(): pl.pallas_call(functools.partial(kernel, image + text_total), out_shape=[...  103 us

profile of v4, /device:TPU:0, one launch (start us, length us, event | category | flops | bytes accessed | tf_op | source)
XLA Modules:
  0.0 105.8 jit_solution(15179249015653821315)
XLA Ops:
  0.6 103.5 %shard_map.104 = (f32[64,512]{1,0:T(8,128)}, f32[64,512]{1,0:T(8,128)}) custom-call(f32[64,512]{1,0:T(8,128)} %bitcast.9, bf16[64,2432]{1,0:T(8,128)(2,1)} %w_embed_hbm.1, bf16[1024,2432]{1,0:T(8,128)(2,1)} %pos_hbm.1, f32[3,64,2432]{2,1,0:T(8,128)} %bitcast.6, s32[1,2]{1,0:T(1,128)} %mod_index.1, bf16[3,2432,768]{2,1,0:T(8,128)(2,1)} %bitcast.5, ...), custom_call_target="tpu_custom_call" | custom-call | tf_op jit(solution)/shard_map/pallas_call | solution.py:432
  104.1 1.7 %shard_map.105 = (f32[1,64,512]{2,1,0:T(8,128)}, f32[1,64,512]{2,1,0:T(8,128)}) custom-call(f32[64,512]{1,0:T(8,128)} %get-tuple-element.4.corrected, f32[64,512]{1,0:T(8,128)} %get-tuple-element.5.first_velocity), custom_call_target="tpu_custom_call" | custom-call | tf_op jit(solution)/shard_map/pallas_call | solution.py:499
